TPU v7x, 32 devices: a whole 2x2x4 slice. The times are simulated.
32 devices in a mesh: mem: 2 (over x), tx: 4 (over z), ty: 4 (over y, core).
Axes of the slice: x: 2, y: 2, z: 4, core: 2. Of those that a mesh axis runs over, the one named last changes fastest.
Arguments:
- pressure: float32 [16, 1024, 1024], P('mem', 'tx', 'ty'), may hold values from -6 to 6
- elevation: float32 [1024, 1024], P('tx', 'ty'), may hold values from -4 to 4
- ks_field: float32 [1024, 1024], P('tx', 'ty'), may hold values from 0.03 to 0.24
- melt_rate: float32 [16, 1024, 1024], P('mem', 'tx', 'ty'), may hold values from -1.5 to 1.5
- obs_index: int32 [1024], replicated, may hold values from 0 to 1048575
- obs_value: float32 [1024], P(('tx', 'ty')), may hold values from -6 to 6
- obs_error: float32 [1024], P(('tx', 'ty')), may hold values from 0.3 to 1
- perturbation: float32 [1024, 16], P(('tx', 'ty'), 'mem'), may hold values from -6 to 6
Outputs:
- analysis: float32 [16, 1024, 1024], P('mem', 'tx', 'ty')
All inputs are finite; a program needn't handle non-finite values.
Results may differ from a plain program's by a relative error of at most 0.0089.
Values may be sent and summed in bfloat16 or wider, within the bound.
A program may use at most 128 MiB of HBM per device.

v0:
```python
import functools

import jax
import jax.numpy as jnp
from jax import lax
from jax.experimental import pallas as pl
from jax.experimental.pallas import tpu as pltpu
from jax.sharding import PartitionSpec as P

SUBSTEPS = 4
HALO = 8
PAD = 2 * HALO
STRIP = 4
CHUNK = 64
F32 = jnp.float32
BF16 = jnp.bfloat16


def kernel(
    n_mem, n_tx, n_ty, share,
    p_hbm, e_hbm, k_hbm, m_hbm, place, packed,
    out,
    p_ext, m_ext, e_ext, k_ext, ping, edges, faces, hot, fore, obs, picks, sums,
    load_sem, row_send, row_recv, edge_send, edge_recv, obs_send, obs_recv,
    fore_send, fore_recv, pick_send, pick_recv, sum_send, sum_recv,
):
    members, size_x, size_y = out.shape
    total = n_mem * members
    n_plane = n_tx * n_ty
    rows = size_x + 2 * PAD
    own = pl.ds(PAD, size_x)
    me_mem = lax.axis_index("mem")
    tx = lax.axis_index("tx")
    ty = lax.axis_index("ty")
    me = tx * n_ty + ty

    def plane(step):
        other = lax.rem(me + step, n_plane)
        return {"tx": other // n_ty, "ty": lax.rem(other, n_ty)}

    def partner(step):
        return {"mem": lax.rem(me_mem + step, n_mem)}

    barrier = pltpu.get_barrier_semaphore()

    def greet(step, carry):
        pl.semaphore_signal(barrier, inc=1, device_id=plane(step))
        return carry

    lax.fori_loop(1, n_plane, greet, 0)
    for step in range(1, n_mem):
        pl.semaphore_signal(barrier, inc=1, device_id=partner(step))

    loads = [
        pltpu.make_async_copy(p_hbm, p_ext.at[:, own, :], load_sem.at[0]),
        pltpu.make_async_copy(m_hbm, m_ext.at[:, own, :], load_sem.at[1]),
        pltpu.make_async_copy(e_hbm, e_ext.at[own, :], load_sem.at[2]),
        pltpu.make_async_copy(k_hbm, k_ext.at[own, :], load_sem.at[3]),
    ]
    for load in loads:
        load.start()
    obs[me] = packed[...]
    pl.semaphore_wait(barrier, n_plane - 1 + n_mem - 1)

    ends = (
        (pl.ds(0, HALO), pl.ds(PAD + size_x, HALO)),
        (pl.ds(size_x - HALO, HALO), pl.ds(HALO, HALO)),
    )

    def row_copies(way):
        source, target = ends[way]
        device = {"tx": tx + (2 * way - 1)}
        pairs = (
            (p_hbm.at[:, source, :], p_ext.at[:, target, :]),
            (m_hbm.at[:, source, :], m_ext.at[:, target, :]),
            (e_hbm.at[source, :], e_ext.at[target, :]),
            (k_hbm.at[source, :], k_ext.at[target, :]),
        )
        return [
            pltpu.make_async_remote_copy(
                src_ref=a, dst_ref=b, send_sem=row_send.at[way, i],
                recv_sem=row_recv.at[way, i], device_id=device,
            )
            for i, (a, b) in enumerate(pairs)
        ]

    send_up, send_down = tx > 0, tx < n_tx - 1
    for way, there in ((0, send_up), (1, send_down)):
        @pl.when(there)
        def _(way=way):
            for copy in row_copies(way):
                copy.start()

    for load in loads:
        load.wait()

    lane = lax.broadcasted_iota(jnp.int32, (1, 128), 1)
    half = 8 * members
    column = lane & 7
    side0 = lane < half
    own_lane = (side0 & (column >= STRIP)) | ((lane >= half) & (column < STRIP))

    def put(base, value, start, source):
        moved = pltpu.roll(value, (start - source) % 128, 1)
        return jnp.where((lane >= start) & (lane < start + STRIP), moved, base)

    def pack(base, first, second, m):
        base = put(base, first[0], 8 * m + STRIP, 0)
        base = put(base, first[1], half + 8 * m, 128 - STRIP)
        base = put(base, second[0], half + 8 * m + STRIP, 0)
        return put(base, second[1], 8 * m, 128 - STRIP)

    def tiles(ref, *at):
        return ref[(*at, own, pl.ds(0, 128))], ref[(*at, own, pl.ds(size_y - 128, 128))]

    base = jnp.zeros((size_x, 128), F32)
    for m in range(members):
        base = pack(base, tiles(p_ext, m), tiles(m_ext, m), m)
    edges[1, 0, own, :] = base
    base = pack(jnp.zeros((size_x, 128), F32), tiles(e_ext), tiles(k_ext), 0)
    width = 8
    while width < half:
        base = base + pltpu.roll(base, width, 1)
        width *= 2
    edges[1, 1, own, :] = base

    spans = {
        -1: (pl.ds(PAD, HALO), pl.ds(PAD + size_x, HALO)),
        0: (own, own),
        1: (pl.ds(PAD + size_x - HALO, HALO), pl.ds(HALO, HALO)),
    }
    around = [(dx, dy) for dx in (-1, 0, 1) for dy in (-1, 0, 1) if (dx, dy) != (0, 0)]

    def inside(dx, dy):
        x, y = tx + dx, ty + dy
        return (x >= 0) & (x < n_tx) & (y >= 0) & (y < n_ty)

    def edge_copy(i):
        dx, dy = around[i]
        source, target = spans[dx]
        return pltpu.make_async_remote_copy(
            src_ref=edges.at[1, :, source, :], dst_ref=edges.at[1 - dy, :, target, :],
            send_sem=edge_send.at[i], recv_sem=edge_recv.at[i],
            device_id={"tx": tx + dx, "ty": ty + dy},
        )

    for i, (dx, dy) in enumerate(around):
        @pl.when(inside(dx, dy))
        def _(i=i):
            edge_copy(i).start()

    def obs_copy(step):
        return pltpu.make_async_remote_copy(
            src_ref=obs.at[me], dst_ref=obs.at[me], send_sem=obs_send.at[step],
            recv_sem=obs_recv.at[step], device_id=plane(step),
        )

    def obs_start(step, carry):
        obs_copy(step).start()
        return carry

    lax.fori_loop(1, n_plane, obs_start, 0)

    n_obs = place.shape[1]
    local_x = place[0:1, :]
    local_y = place[1:2, :]
    hot[...] = jnp.where(
        lax.broadcasted_iota(jnp.int32, (size_y, n_obs), 0) == local_y, F32(1), F32(0)
    ).astype(BF16)

    for way, there, back in ((0, send_up, send_down), (1, send_down, send_up)):
        @pl.when(there)
        def _(way=way):
            for copy in row_copies(way):
                copy.wait_send()

        @pl.when(back)
        def _(way=way):
            for copy in row_copies(way):
                copy.wait_recv()
    for i, (dx, dy) in enumerate(around):
        @pl.when(inside(dx, dy))
        def _(i=i):
            edge_copy(i).wait_send()

        @pl.when(inside(-dx, -dy))
        def _(i=i):
            edge_copy(i).wait_recv()

    k_ext[...] = 0.25 * k_ext[...]

    def unpack(i):
        left, mine, right = edges[0, i], edges[1, i], edges[2, i]
        beside = jnp.where(side0, pltpu.roll(left, half, 1), pltpu.roll(right, half, 1))
        second = jnp.where(own_lane, pltpu.roll(mine, half, 1), jnp.where(side0, left, right))
        return jnp.where(own_lane, mine, beside), second

    pres, melt = unpack(0)
    elev, quarter = unpack(1)
    quarter = 0.25 * quarter
    column_global = ty * size_y + column + jnp.where(side0, -STRIP, size_y - STRIP)
    right_in = (column_global >= 0) & (column_global < n_ty * size_y - 1)

    def down_in(first, count, lanes):
        at = lax.broadcasted_iota(jnp.int32, (count, lanes), 0) + (first - PAD) + tx * size_x
        return (at >= 0) & (at < n_tx * size_x - 1)

    for t in range(SUBSTEPS):
        cond = quarter + quarter * jnp.tanh(0.5 * pres)
        head = pres + elev
        over = jnp.where(
            right_in,
            (cond + pltpu.roll(cond, 127, 1)) * (pltpu.roll(head, 127, 1) - head), F32(0),
        )
        faces[t] = over
        if t < SUBSTEPS - 1:
            down = jnp.where(
                down_in(0, rows, 128),
                (cond + pltpu.roll(cond, rows - 1, 0)) * (pltpu.roll(head, rows - 1, 0) - head),
                F32(0),
            )
            pres = pres + (over - pltpu.roll(over, 1, 1)) + (down - pltpu.roll(down, 1, 0)) + melt

    inner = list(range(PAD, PAD + size_x, CHUNK)) + [PAD + size_x]
    wide = [HALO] + inner[1:-1] + [PAD + size_x + HALO]

    def fore_copy(step, m):
        return pltpu.make_async_remote_copy(
            src_ref=fore.at[me_mem, m], dst_ref=fore.at[me_mem, m],
            send_sem=fore_send.at[step, m], recv_sem=fore_recv.at[step, m],
            device_id=partner(step),
        )

    def member(m, carry):
        for t in range(SUBSTEPS):
            cuts = wide if t < SUBSTEPS - 1 else inner
            for a, b in zip(cuts[:-1], cuts[1:]):
                count = b - a + 2 * HALO
                span = pl.ds(a - HALO, count)
                p = p_ext[m, span, :] if t == 0 else ping[(t - 1) % 2, span, :]
                k = k_ext[span, :]
                cond = k + k * jnp.tanh(0.5 * p)
                head = p + e_ext[span, :]
                down = (cond + pltpu.roll(cond, count - 1, 0)) * (
                    pltpu.roll(head, count - 1, 0) - head
                )
                if a <= PAD or b >= PAD + size_x:
                    down = jnp.where(down_in(a - HALO, count, size_y), down, F32(0))
                upright = (down - pltpu.roll(down, 1, 0))[HALO : count - HALO]
                c, h = cond[HALO : count - HALO], head[HALO : count - HALO]
                over = (c + pltpu.roll(c, size_y - 1, 1)) * (pltpu.roll(h, size_y - 1, 1) - h)
                face = faces[t, pl.ds(a, b - a), :]
                low = pltpu.roll(face, 128 - (STRIP - 1) - 8 * m, 1)
                high = pltpu.roll(face, 128 - half - STRIP - 8 * m, 1)
                over = jnp.concatenate(
                    [over[:, :-128], jnp.where(lane == 127, high, over[:, -128:])], axis=1
                )
                back = pltpu.roll(over, 1, 1)
                back = jnp.concatenate(
                    [jnp.where(lane == 0, low, back[:, :128]), back[:, 128:]], axis=1
                )
                new = (
                    p[HALO : count - HALO] + (over - back) + upright
                    + m_ext[m, pl.ds(a, b - a), :]
                )
                if t < SUBSTEPS - 1:
                    ping[t % 2, pl.ds(a, b - a), :] = new
                else:
                    out[m, pl.ds(a - PAD, b - a), :] = new
                    fore[me_mem, m, pl.ds(a - PAD, b - a), :] = new.astype(BF16)
        for step in range(1, n_mem):
            fore_copy(step, m).start()
        value = out[m]
        top = value.astype(BF16)
        rest = (value - top.astype(F32)).astype(BF16)
        piece = 256 if n_obs % 256 == 0 else n_obs
        row = lax.broadcasted_iota(jnp.int32, (size_x, piece), 0)
        for at in range(0, n_obs, piece):
            some = hot[:, at : at + piece]
            got = jnp.dot(top, some, preferred_element_type=F32) + jnp.dot(
                rest, some, preferred_element_type=F32
            )
            got = jnp.where(row == local_x[:, at : at + piece], got, F32(0))
            picks[pl.ds(me_mem * members + m, 1), at : at + piece] = jnp.sum(
                got, axis=0, keepdims=True
            )
        return carry

    lax.fori_loop(0, members, member, 0)

    mine = pl.ds(pl.multiple_of(me_mem * members, 8), members)

    def pick_copy(step):
        return pltpu.make_async_remote_copy(
            src_ref=picks.at[mine, :], dst_ref=picks.at[mine, :],
            send_sem=pick_send.at[step], recv_sem=pick_recv.at[step], device_id=partner(step),
        )

    for step in range(1, n_mem):
        pick_copy(step).start()

    def obs_wait(step, carry):
        obs_copy(step).wait()
        return carry

    lax.fori_loop(1, n_plane, obs_wait, 0)
    per = 128 // share
    parts = []
    for first in range(0, n_plane, per):
        part = obs[first]
        for j in range(1, per):
            part = part + pltpu.roll(obs[first + j], j * share, 1)
        parts.append(part)
    every = jnp.concatenate(parts, axis=1)
    noise, value, error = every[:members], every[members : members + 1], every[members + 1 : members + 2]
    here = (local_x >= 0) & (local_x < size_x) & (local_y >= 0) & (local_y < size_y)

    for step in range(1, n_mem):
        pick_copy(step).wait()
    innovation = (value + error * noise - picks[mine, :]) / error
    seen = picks[...]
    anomaly = (seen - jnp.mean(seen, axis=0, keepdims=True)) / error
    anomaly = jnp.where(here, anomaly, F32(0))
    lanes = sums.shape[2]
    both = jnp.concatenate(
        [anomaly, innovation, jnp.zeros((lanes - total - members, n_obs), F32)], axis=0
    )
    sums[me] = lax.dot_general(
        anomaly, both, (((1,), (1,)), ((), ())),
        precision=lax.Precision.HIGHEST, preferred_element_type=F32,
    )

    def sum_copy(step):
        return pltpu.make_async_remote_copy(
            src_ref=sums.at[me], dst_ref=sums.at[me], send_sem=sum_send.at[step],
            recv_sem=sum_recv.at[step], device_id=plane(step),
        )

    def sum_start(step, carry):
        sum_copy(step).start()
        return carry

    def sum_wait(step, carry):
        sum_copy(step).wait()
        return carry

    lax.fori_loop(1, n_plane, sum_start, 0)
    lax.fori_loop(1, n_plane, sum_wait, 0)
    ri = lax.broadcasted_iota(jnp.int32, (total, lanes), 0)
    ci = lax.broadcasted_iota(jnp.int32, (total, lanes), 1)
    system = jnp.sum(sums[...], axis=0) + jnp.where(ri == ci, F32(total - 1), F32(0))
    for k in range(total):
        pivot = system[k : k + 1, :] / system[k : k + 1, k : k + 1]
        system = jnp.where(ri == k, pivot, system - system[:, k : k + 1] * pivot)
    weights = system.astype(BF16)

    group = 16
    ra = lax.broadcasted_iota(jnp.int32, (members * group, lanes), 0)
    rb = lax.broadcasted_iota(jnp.int32, (members * group, lanes), 1)
    choose = jnp.where(rb - total == ra // group, F32(1), F32(0)).astype(BF16)
    spread = lax.dot_general(
        choose, weights, (((1,), (1,)), ((), ())), preferred_element_type=F32
    ).astype(BF16)
    ca = lax.broadcasted_iota(jnp.int32, (total, total * group), 0)
    cb = lax.broadcasted_iota(jnp.int32, (total, total * group), 1)
    repeat = jnp.where(cb // group == ca, F32(1), F32(0)).astype(BF16)
    spread = jnp.dot(spread, repeat, preferred_element_type=F32)
    da = lax.broadcasted_iota(jnp.int32, spread.shape, 0)
    db = lax.broadcasted_iota(jnp.int32, spread.shape, 1)
    spread = jnp.where((da & (group - 1)) == (db & (group - 1)), spread, F32(0)).astype(BF16)

    def fore_wait(m, carry):
        for step in range(1, n_mem):
            fore_copy(step, m).wait()
        return carry

    lax.fori_loop(0, members, fore_wait, 0)

    def finish(g, carry):
        span = pl.ds(pl.multiple_of(g * group, group), group)
        block = fore[:, :, span, :].reshape(total * group, size_y)
        shift = jnp.dot(spread, block, preferred_element_type=F32)
        out[:, span, :] = out[:, span, :] + shift.reshape(members, group, size_y)
        return carry

    lax.fori_loop(0, size_x // group, finish, 0)


def local(pressure, elevation, ks_field, melt_rate, obs_index, obs_value, obs_error, perturbation):
    members, size_x, size_y = pressure.shape
    n_mem, n_tx, n_ty = (lax.axis_size(a) for a in ("mem", "tx", "ty"))
    n_plane = n_tx * n_ty
    total = n_mem * members
    share = obs_value.shape[0]
    n_obs = obs_index.shape[0]
    total_y = size_y * n_ty
    place = jnp.stack(
        [
            obs_index // total_y - lax.axis_index("tx") * size_x,
            obs_index % total_y - lax.axis_index("ty") * size_y,
        ]
    )
    packed = jnp.concatenate([perturbation.T, obs_value[None], obs_error[None]], axis=0)
    height = -(-(members + 2) // 8) * 8
    packed = jnp.pad(packed, ((0, height - members - 2), (0, 128 - share)))
    lanes = -(-(total + members) // 128) * 128
    rows = size_x + 2 * PAD
    dma = pltpu.SemaphoreType.DMA
    vmem = pl.BlockSpec(memory_space=pltpu.VMEM)
    hbm = pl.BlockSpec(memory_space=pl.ANY)
    return pl.pallas_call(
        functools.partial(kernel, n_mem, n_tx, n_ty, share),
        out_shape=jax.ShapeDtypeStruct(pressure.shape, F32),
        in_specs=[hbm] * 4 + [vmem] * 2,
        out_specs=vmem,
        scratch_shapes=[
            pltpu.VMEM((members, rows, size_y), F32),
            pltpu.VMEM((members, rows, size_y), F32),
            pltpu.VMEM((rows, size_y), F32),
            pltpu.VMEM((rows, size_y), F32),
            pltpu.VMEM((2, rows, size_y), F32),
            pltpu.VMEM((3, 2, rows, 128), F32),
            pltpu.VMEM((SUBSTEPS, rows, 128), F32),
            pltpu.VMEM((size_y, n_obs), BF16),
            pltpu.VMEM((n_mem, members, size_x, size_y), BF16),
            pltpu.VMEM((n_plane, height, 128), F32),
            pltpu.VMEM((total, n_obs), F32),
            pltpu.VMEM((n_plane, total, lanes), F32),
            dma((4,)), dma((2, 4)), dma((2, 4)), dma((8,)), dma((8,)),
            dma((n_plane,)), dma((n_plane,)),
            dma((n_mem, members)), dma((n_mem, members)),
            dma((n_mem,)), dma((n_mem,)), dma((n_plane,)), dma((n_plane,)),
        ],
        compiler_params=pltpu.CompilerParams(
            collective_id=0, has_side_effects=True, vmem_limit_bytes=48 * 2**20
        ),
    )(pressure, elevation, ks_field, melt_rate, place, packed)


def solution(mesh):
    placed = (
        P("mem", "tx", "ty"),
        P("tx", "ty"),
        P("tx", "ty"),
        P("mem", "tx", "ty"),
        P(),
        P(("tx", "ty")),
        P(("tx", "ty")),
        P(("tx", "ty"), "mem"),
    )
    return jax.shard_map(
        local, mesh=mesh, in_specs=placed, out_specs=P("mem", "tx", "ty"), check_vma=False
    )
```

profile of v0, /device:TPU:0, one launch (start us, length us, event | category | flops | bytes accessed | tf_op | source)
XLA Modules:
  0.0 56.5 jit_solution(5547619344481306965)
XLA Ops:
  0.0 0.7 %fusion = (s32[1024]{0:T(1024)S(1)}, s32[1024]{0:T(1024)S(1)}) fusion(s32[1024]{0:T(1024)} %param.12, s32[]{:T(128)S(6)} %mul.6, s32[]{:T(128)S(6)} %mul.7), kind=kLoop, calls=%fused_computation.10 | loop fusion | flops 21504 | bytes 12296 | tf_op jit(solution)/shard_map/sub | solution.py:399
  0.7 0.7 %select_maximum_fusion.packed = f32[16,128]{1,0:T(8,128)S(1)} fusion(f32[1,64]{1,0:T(1,128)} %bitcast.8, f32[1,64]{1,0:T(1,128)} %bitcast.9, f32[8,64]{1,0:T(8,128)} %bitcast.7), kind=kLoop, calls=%fused_computation | loop fusion | flops 22528 | bytes 10752 | tf_op jit(solution)/shard_map/concatenate | solution.py:403
  1.4 0.0 copy-start
  1.5 1.6 %copy-done = f32[8,256,256]{2,1,0:T(8,128)S(1)} copy-done((f32[8,256,256]{2,1,0:T(8,128)S(1)}, f32[8,256,256]{2,1,0:T(8,128)}, u32[]{:S(2)}) %copy-start) | copy-done | bytes 2097176
  3.0 0.0 copy-start.1
  3.0 0.9 %copy-done.1 = f32[256,256]{1,0:T(8,128)S(1)} copy-done((f32[256,256]{1,0:T(8,128)S(1)}, f32[256,256]{1,0:T(8,128)}, u32[]{:S(2)}) %copy-start.1) | copy-done | bytes 262168
  4.0 0.0 copy-start.2
  4.0 0.9 %copy-done.2 = f32[256,256]{1,0:T(8,128)S(1)} copy-done((f32[256,256]{1,0:T(8,128)S(1)}, f32[256,256]{1,0:T(8,128)}, u32[]{:S(2)}) %copy-start.2) | copy-done | bytes 262168
  4.9 50.2 %shard_map.82 = f32[8,256,256]{2,1,0:T(8,128)S(1)} custom-call(f32[8,256,256]{2,1,0:T(8,128)S(1)} %copy-done, f32[256,256]{1,0:T(8,128)S(1)} %copy-done.1, f32[256,256]{1,0:T(8,128)S(1)} %copy-done.2, f32[8,256,256]{2,1,0:T(8,128)} %m_hbm.1, s32[2,1024]{1,0:T(2,128)S(1)} %pad_add_fusion.place, f32[16,128]{1,0:T(8,128)S(1)} %select_maximum_fusion.packed), custom_call_target="tpu_custom_call" | custom-call | tf_op jit(solution)/shard_map/pallas_call | solution.py:411
  55.1 1.3 %copy.10 = f32[8,256,256]{2,1,0:T(8,128)} copy(f32[8,256,256]{2,1,0:T(8,128)S(1)} %shard_map.82) | data formatting | bytes 4194304
  (1 shorter events, 0.0 us)
Async XLA Ops:
  1.4 1.6 %copy-start = (f32[8,256,256]{2,1,0:T(8,128)S(1)}, f32[8,256,256]{2,1,0:T(8,128)}, u32[]{:S(2)}) copy-start(f32[8,256,256]{2,1,0:T(8,128)} %p_hbm.1) | copy-start | bytes 6291460
  3.0 0.9 %copy-start.1 = (f32[256,256]{1,0:T(8,128)S(1)}, f32[256,256]{1,0:T(8,128)}, u32[]{:S(2)}) copy-start(f32[256,256]{1,0:T(8,128)} %e_hbm.1) | copy-start | bytes 786436
  4.0 0.9 %copy-start.2 = (f32[256,256]{1,0:T(8,128)S(1)}, f32[256,256]{1,0:T(8,128)}, u32[]{:S(2)}) copy-start(f32[256,256]{1,0:T(8,128)} %k_hbm.1) | copy-start | bytes 786436
where the time goes:
time: 56.7 us; the launch traced here: 56.5 us
  Pallas kernels  50.2 us (89%)
  local copies, waits for them, and re-layouts  4.81 us (8%)
  other arithmetic  1.44 us (3%)
    pallas_call x1, Pallas kernels, local(): pl.pallas_call(functools.partial(kernel, n_mem, n_tx, n_ty, share), out_s...  50.2 us
    unnamed x7, local copies, waits for them, and re-layouts  4.81 us

commit v1 on v0

--- a/solution.py
+++ b/solution.py
@@ -12,15 +12,17 @@
 PAD = 2 * HALO
 STRIP = 4
 CHUNK = 64
+LATE = 2
 F32 = jnp.float32
 BF16 = jnp.bfloat16
 
 
 def kernel(
     n_mem, n_tx, n_ty, share,
-    p_hbm, e_hbm, k_hbm, m_hbm, place, packed,
+    p_hbm, e_hbm, k_hbm, m_hbm, index_hbm, value_hbm, error_hbm, noise_hbm,
     out,
     p_ext, m_ext, e_ext, k_ext, ping, edges, faces, hot, fore, obs, picks, sums,
+    index, own_value, own_error, own_noise,
     load_sem, row_send, row_recv, edge_send, edge_recv, obs_send, obs_recv,
     fore_send, fore_recv, pick_send, pick_recv, sum_send, sum_recv,
 ):
@@ -57,9 +59,15 @@
         pltpu.make_async_copy(e_hbm, e_ext.at[own, :], load_sem.at[2]),
         pltpu.make_async_copy(k_hbm, k_ext.at[own, :], load_sem.at[3]),
     ]
-    for load in loads:
+    small = [
+        pltpu.make_async_copy(index_hbm, index, load_sem.at[4]),
+        pltpu.make_async_copy(value_hbm, own_value, load_sem.at[5]),
+        pltpu.make_async_copy(error_hbm, own_error, load_sem.at[6]),
+        pltpu.make_async_copy(noise_hbm, own_noise, load_sem.at[7]),
+    ]
+    for load in loads + small:
         load.start()
-    obs[me] = packed[...]
+    obs[me] = jnp.zeros(obs.shape[1:], F32)
     pl.semaphore_wait(barrier, n_plane - 1 + n_mem - 1)
 
     ends = (
@@ -159,11 +167,21 @@
         obs_copy(step).start()
         return carry
 
+    for load in small:
+        load.wait()
+    obs[me, :members, :share] = own_noise[...]
+    obs[me, members : members + 1, :share] = own_value[...]
+    obs[me, members + 1 : members + 2, :share] = own_error[...]
     lax.fori_loop(1, n_plane, obs_start, 0)
 
-    n_obs = place.shape[1]
-    local_x = place[0:1, :]
-    local_y = place[1:2, :]
+    n_obs = index.shape[1]
+    total_y = n_ty * size_y
+    if total_y & (total_y - 1):
+        global_x = index[...] // total_y
+    else:
+        global_x = lax.shift_right_logical(index[...], total_y.bit_length() - 1)
+    local_x = global_x - tx * size_x
+    local_y = index[...] - global_x * total_y - ty * size_y
     hot[...] = jnp.where(
         lax.broadcasted_iota(jnp.int32, (size_y, n_obs), 0) == local_y, F32(1), F32(0)
     ).astype(BF16)
@@ -268,8 +286,11 @@
                 else:
                     out[m, pl.ds(a - PAD, b - a), :] = new
                     fore[me_mem, m, pl.ds(a - PAD, b - a), :] = new.astype(BF16)
-        for step in range(1, n_mem):
-            fore_copy(step, m).start()
+        @pl.when(m < members - LATE)
+        def _():
+            for step in range(1, n_mem):
+                fore_copy(step, m).start()
+
         value = out[m]
         top = value.astype(BF16)
         rest = (value - top.astype(F32)).astype(BF16)
@@ -298,6 +319,9 @@
 
     for step in range(1, n_mem):
         pick_copy(step).start()
+    for m in range(members - LATE, members):
+        for step in range(1, n_mem):
+            fore_copy(step, m).start()
 
     def obs_wait(step, carry):
         obs_copy(step).wait()
@@ -393,25 +417,16 @@
     total = n_mem * members
     share = obs_value.shape[0]
     n_obs = obs_index.shape[0]
-    total_y = size_y * n_ty
-    place = jnp.stack(
-        [
-            obs_index // total_y - lax.axis_index("tx") * size_x,
-            obs_index % total_y - lax.axis_index("ty") * size_y,
-        ]
-    )
-    packed = jnp.concatenate([perturbation.T, obs_value[None], obs_error[None]], axis=0)
     height = -(-(members + 2) // 8) * 8
-    packed = jnp.pad(packed, ((0, height - members - 2), (0, 128 - share)))
     lanes = -(-(total + members) // 128) * 128
     rows = size_x + 2 * PAD
     dma = pltpu.SemaphoreType.DMA
     vmem = pl.BlockSpec(memory_space=pltpu.VMEM)
-    hbm = pl.BlockSpec(memory_space=pl.ANY)
+    hbm = pl.BlockSpec(memory_space=pltpu.HBM)
     return pl.pallas_call(
         functools.partial(kernel, n_mem, n_tx, n_ty, share),
         out_shape=jax.ShapeDtypeStruct(pressure.shape, F32),
-        in_specs=[hbm] * 4 + [vmem] * 2,
+        in_specs=[hbm] * 8,
         out_specs=vmem,
         scratch_shapes=[
             pltpu.VMEM((members, rows, size_y), F32),
@@ -426,15 +441,22 @@
             pltpu.VMEM((n_plane, height, 128), F32),
             pltpu.VMEM((total, n_obs), F32),
             pltpu.VMEM((n_plane, total, lanes), F32),
-            dma((4,)), dma((2, 4)), dma((2, 4)), dma((8,)), dma((8,)),
+            pltpu.VMEM((1, n_obs), jnp.int32),
+            pltpu.VMEM((1, share), F32),
+            pltpu.VMEM((1, share), F32),
+            pltpu.VMEM((members, share), F32),
+            dma((8,)), dma((2, 4)), dma((2, 4)), dma((8,)), dma((8,)),
             dma((n_plane,)), dma((n_plane,)),
             dma((n_mem, members)), dma((n_mem, members)),
             dma((n_mem,)), dma((n_mem,)), dma((n_plane,)), dma((n_plane,)),
         ],
         compiler_params=pltpu.CompilerParams(
-            collective_id=0, has_side_effects=True, vmem_limit_bytes=48 * 2**20
+            collective_id=0, has_side_effects=True, vmem_limit_bytes=57 * 2**20
         ),
-    )(pressure, elevation, ks_field, melt_rate, place, packed)
+    )(
+        pressure, elevation, ks_field, melt_rate,
+        obs_index[None], obs_value[None], obs_error[None], perturbation.T,
+    )
 
 
 def solution(mesh):

time: 56.7 us -> 50.2 us (0.89)
  Pallas kernels: 50.2 us -> 47 us
  local copies, waits for them, and re-layouts: 4.81 us -> 3.05 us
  other arithmetic: 1.44 us -> 0 us
    pallas_call x1, Pallas kernels: 50.2 us -> 47 us  [local(): pl.pallas_call(functools.partial(kernel, n_mem, n_tx, n_ty, share), out_s...]
    unnamed x7 -> x1, local copies, waits for them, and re-layouts: 4.81 us -> 3.05 us
    concatenate x1 -> x0, other arithmetic: 0.73 us -> none  [local(): jnp.concatenate([perturbation.T, obs_value[None], obs_error[None]], axis=0)]
    sub x1 -> x0, other arithmetic: 0.7 us -> none  [local(): obs_index // total_y - lax.axis_index('tx') * size_x]
where the time goes in v1:
time: 50.2 us; the launch traced here: 50.1 us
  Pallas kernels  47 us (94%)
  local copies, waits for them, and re-layouts  3.05 us (6%)
    pallas_call x1, Pallas kernels, local(): pl.pallas_call(functools.partial(kernel, n_mem, n_tx, n_ty, share), out_s...  47 us
    unnamed x1, local copies, waits for them, and re-layouts  3.05 us

profile of v1, /device:TPU:0, one launch (start us, length us, event | category | flops | bytes accessed | tf_op | source)
XLA Modules:
  0.0 50.1 jit_solution(15010062668441647790)
XLA Ops:
  0.0 47.0 %shard_map.82 = f32[8,256,256]{2,1,0:T(8,128)} custom-call(f32[8,256,256]{2,1,0:T(8,128)} %p_hbm.1, f32[256,256]{1,0:T(8,128)} %e_hbm.1, f32[256,256]{1,0:T(8,128)} %k_hbm.1, f32[8,256,256]{2,1,0:T(8,128)} %m_hbm.1, s32[1,1024]{1,0:T(1,128)} %bitcast.4, f32[1,64]{1,0:T(1,128)} %bitcast.6, f32[1,64]{1,0:T(1,128)} %bitcast.7, f32[8,64]{1,0:T(8,128)} %bitcast.5), custom_call_target="tpu_custom_call" | custom-call | tf_op jit(solution)/shard_map/pallas_call | solution.py:426
  47.0 3.0 %copy.10 = f32[8,256,256]{2,1,0:T(8,128)} copy(f32[8,256,256]{2,1,0:T(8,128)} %shard_map.82) | data formatting | bytes 4194304

commit v2 on v1

--- a/solution.py
+++ b/solution.py
@@ -12,7 +12,8 @@
 PAD = 2 * HALO
 STRIP = 4
 CHUNK = 64
-LATE = 2
+SLABS = 4
+LATE = 3
 F32 = jnp.float32
 BF16 = jnp.bfloat16
 
@@ -20,11 +21,11 @@
 def kernel(
     n_mem, n_tx, n_ty, share,
     p_hbm, e_hbm, k_hbm, m_hbm, index_hbm, value_hbm, error_hbm, noise_hbm,
-    out,
-    p_ext, m_ext, e_ext, k_ext, ping, edges, faces, hot, fore, obs, picks, sums,
+    out_hbm,
+    out, p_ext, m_ext, e_ext, k_ext, ping, edges, faces, hot, fore, obs, picks, sums,
     index, own_value, own_error, own_noise,
     load_sem, row_send, row_recv, edge_send, edge_recv, obs_send, obs_recv,
-    fore_send, fore_recv, pick_send, pick_recv, sum_send, sum_recv,
+    fore_send, fore_recv, late_send, late_recv, pick_send, pick_recv, sum_send, sum_recv,
 ):
     members, size_x, size_y = out.shape
     total = n_mem * members
@@ -49,7 +50,8 @@
         pl.semaphore_signal(barrier, inc=1, device_id=plane(step))
         return carry
 
-    lax.fori_loop(1, n_plane, greet, 0)
+    for step in range(1, n_plane):
+        greet(step, 0)
     for step in range(1, n_mem):
         pl.semaphore_signal(barrier, inc=1, device_id=partner(step))
 
@@ -311,6 +313,8 @@
 
     mine = pl.ds(pl.multiple_of(me_mem * members, 8), members)
 
+    group = 16
+
     def pick_copy(step):
         return pltpu.make_async_remote_copy(
             src_ref=picks.at[mine, :], dst_ref=picks.at[mine, :],
@@ -319,9 +323,22 @@
 
     for step in range(1, n_mem):
         pick_copy(step).start()
-    for m in range(members - LATE, members):
+    slabs = SLABS
+    per_slab = size_x // group // slabs
+
+    def slab_rows(i):
+        return pl.ds(i * per_slab * group, per_slab * group)
+
+    def late_copy(step, i):
+        piece = fore.at[me_mem, pl.ds(members - LATE, LATE), slab_rows(i), :]
+        return pltpu.make_async_remote_copy(
+            src_ref=piece, dst_ref=piece, send_sem=late_send.at[step, i],
+            recv_sem=late_recv.at[step, i], device_id=partner(step),
+        )
+
+    for i in range(slabs):
         for step in range(1, n_mem):
-            fore_copy(step, m).start()
+            late_copy(step, i).start()
 
     def obs_wait(step, carry):
         obs_copy(step).wait()
@@ -378,7 +395,6 @@
         system = jnp.where(ri == k, pivot, system - system[:, k : k + 1] * pivot)
     weights = system.astype(BF16)
 
-    group = 16
     ra = lax.broadcasted_iota(jnp.int32, (members * group, lanes), 0)
     rb = lax.broadcasted_iota(jnp.int32, (members * group, lanes), 1)
     choose = jnp.where(rb - total == ra // group, F32(1), F32(0)).astype(BF16)
@@ -398,7 +414,7 @@
             fore_copy(step, m).wait()
         return carry
 
-    lax.fori_loop(0, members, fore_wait, 0)
+    lax.fori_loop(0, members - LATE, fore_wait, 0)
 
     def finish(g, carry):
         span = pl.ds(pl.multiple_of(g * group, group), group)
@@ -407,7 +423,17 @@
         out[:, span, :] = out[:, span, :] + shift.reshape(members, group, size_y)
         return carry
 
-    lax.fori_loop(0, size_x // group, finish, 0)
+    def leave(i):
+        span = slab_rows(i)
+        return pltpu.make_async_copy(out.at[:, span, :], out_hbm.at[:, span, :], load_sem.at[i])
+
+    for i in range(slabs):
+        for step in range(1, n_mem):
+            late_copy(step, i).wait()
+        lax.fori_loop(i * per_slab, (i + 1) * per_slab, finish, 0)
+        leave(i).start()
+    for i in range(slabs):
+        leave(i).wait()
 
 
 def local(pressure, elevation, ks_field, melt_rate, obs_index, obs_value, obs_error, perturbation):
@@ -421,14 +447,14 @@
     lanes = -(-(total + members) // 128) * 128
     rows = size_x + 2 * PAD
     dma = pltpu.SemaphoreType.DMA
-    vmem = pl.BlockSpec(memory_space=pltpu.VMEM)
     hbm = pl.BlockSpec(memory_space=pltpu.HBM)
     return pl.pallas_call(
         functools.partial(kernel, n_mem, n_tx, n_ty, share),
         out_shape=jax.ShapeDtypeStruct(pressure.shape, F32),
         in_specs=[hbm] * 8,
-        out_specs=vmem,
+        out_specs=hbm,
         scratch_shapes=[
+            pltpu.VMEM(pressure.shape, F32),
             pltpu.VMEM((members, rows, size_y), F32),
             pltpu.VMEM((members, rows, size_y), F32),
             pltpu.VMEM((rows, size_y), F32),
@@ -448,6 +474,7 @@
             dma((8,)), dma((2, 4)), dma((2, 4)), dma((8,)), dma((8,)),
             dma((n_plane,)), dma((n_plane,)),
             dma((n_mem, members)), dma((n_mem, members)),
+            dma((n_mem, SLABS)), dma((n_mem, SLABS)),
             dma((n_mem,)), dma((n_mem,)), dma((n_plane,)), dma((n_plane,)),
         ],
         compiler_params=pltpu.CompilerParams(

time: 50.2 us -> 49.5 us (0.986)
  Pallas kernels: 47 us -> 46.3 us
    pallas_call x1, Pallas kernels: 47 us -> 46.3 us  [local(): pl.pallas_call(functools.partial(kernel, n_mem, n_tx, n_ty, share), out_s...]
where the time goes in v2:
time: 49.5 us; the launch traced here: 49.4 us
  Pallas kernels  46.3 us (94%)
  local copies, waits for them, and re-layouts  3.05 us (6%)
    pallas_call x1, Pallas kernels, local(): pl.pallas_call(functools.partial(kernel, n_mem, n_tx, n_ty, share), out_s...  46.3 us
    unnamed x1, local copies, waits for them, and re-layouts  3.05 us

profile of v2, /device:TPU:0, one launch (start us, length us, event | category | flops | bytes accessed | tf_op | source)
XLA Modules:
  0.0 49.4 jit_solution(9426028604296743141)
XLA Ops:
  0.0 46.3 %shard_map.82 = f32[8,256,256]{2,1,0:T(8,128)} custom-call(f32[8,256,256]{2,1,0:T(8,128)} %p_hbm.1, f32[256,256]{1,0:T(8,128)} %e_hbm.1, f32[256,256]{1,0:T(8,128)} %k_hbm.1, f32[8,256,256]{2,1,0:T(8,128)} %m_hbm.1, s32[1,1024]{1,0:T(1,128)} %bitcast.4, f32[1,64]{1,0:T(1,128)} %bitcast.6, f32[1,64]{1,0:T(1,128)} %bitcast.7, f32[8,64]{1,0:T(8,128)} %bitcast.5), custom_call_target="tpu_custom_call" | custom-call | tf_op jit(solution)/shard_map/pallas_call | solution.py:451
  46.3 3.0 %copy.10 = f32[8,256,256]{2,1,0:T(8,128)} copy(f32[8,256,256]{2,1,0:T(8,128)} %shard_map.82) | data formatting | bytes 4194304
